TPU v7x, 768 devices: a whole 4x8x12 slice. The times are simulated.
768 devices in a mesh: grp: 64 (over y, x, core), loc: 12 (over z).
Axes of the slice: x: 4, y: 8, z: 12, core: 2. Of those that a mesh axis runs over, the one named last changes fastest.
Arguments:
- grad_rows: float32 [786432, 128], P(('grp', 'loc')), may hold values from -24 to 24
- row_owner: int32 [786432, 1], P(('grp', 'loc')), may hold values from 0 to 767; in each aligned block of 1024 rows (0 to 1023, 1024 to 2047, ...) at most 3 rows name the same one
- row_slot: int32 [786432], P(('grp', 'loc')), may hold values from 0 to 1023
- weights: float32 [786432, 128], P(('grp', 'loc')), may hold values from -6 to 6
- first_moment: float32 [786432, 128], P(('grp', 'loc')), may hold values from -6 to 6
- second_moment: float32 [786432, 128], P(('grp', 'loc')), may hold values from 1 to 10
Outputs:
- new_weights: float32 [786432, 128], P(('grp', 'loc'))
- new_first: float32 [786432, 128], P(('grp', 'loc'))
- new_second: float32 [786432, 128], P(('grp', 'loc'))
Inputs may be any that keep to these rules, and one draw needn't show every extreme that they name: `row_owner`: among the rows of one device no owner is named by more than 3 rows, a bound that some block reaches.
All inputs are finite; a program needn't handle non-finite values.
Results may differ from a plain program's by a relative error of at most 0.00005.
Values sent between devices are 32-bit elements; how exact they have to be, the bound alone decides.
A program may use at most 32 MiB of HBM per device.

v0:
```python
import jax
import jax.numpy as jnp
from jax import lax
from jax.sharding import PartitionSpec as P

STEP = 1000


def on_device(grad_rows, row_owner, row_slot, weights, first_moment, second_moment):
    group_count = lax.axis_size("grp")
    local_count = lax.axis_size("loc")
    devices_all = group_count * local_count
    rows, width = grad_rows.shape
    shard = weights.shape[0]
    capacity = max(2, (2 * rows + devices_all - 1) // devices_all)
    owner = row_owner[:, 0]
    same_owner = owner[:, None] == owner[None, :]
    before = lax.broadcasted_iota(jnp.int32, (rows, rows), 1) < lax.broadcasted_iota(
        jnp.int32, (rows, rows), 0
    )
    rank = jnp.sum(jnp.logical_and(same_owner, before).astype(jnp.int32), axis=1)
    position = owner * capacity + rank
    send_grads = jnp.zeros((devices_all * capacity, width), jnp.float32).at[position].set(grad_rows)
    send_slots = jnp.full((devices_all * capacity,), -1, jnp.int32).at[position].set(row_slot)
    send_grads = send_grads.reshape(group_count, local_count, capacity, width)
    send_slots = send_slots.reshape(group_count, local_count, capacity)
    middle = (
        lax.all_to_all(send_grads, "loc", split_axis=1, concat_axis=1, tiled=True),
        lax.all_to_all(send_slots, "loc", split_axis=1, concat_axis=1, tiled=True),
    )
    arrived = (
        lax.all_to_all(middle[0], "grp", split_axis=0, concat_axis=0, tiled=True),
        lax.all_to_all(middle[1], "grp", split_axis=0, concat_axis=0, tiled=True),
    )
    got_grads = arrived[0].reshape(devices_all * capacity, width)
    got_slots = arrived[1].reshape(devices_all * capacity)
    table_index = lax.broadcasted_iota(jnp.int32, (shard, devices_all * capacity), 0)
    selector = (table_index == got_slots[None, :]).astype(jnp.float32)
    summed = jnp.dot(
        selector, got_grads, precision=lax.Precision.HIGHEST, preferred_element_type=jnp.float32
    )
    touched = jnp.sum(selector, axis=1)
    active = (touched > 0.5)[:, None]
    first_next = 0.9 * first_moment + 0.1 * summed
    second_next = 0.99 * second_moment + 0.01 * summed * summed
    first_hat = first_next / (1.0 - 0.9**STEP)
    second_hat = second_next / (1.0 - 0.99**STEP)
    weights_next = weights - 0.5 * first_hat / (jnp.sqrt(second_hat) + 1e-08)
    new_first = jnp.where(active, first_next, first_moment)
    new_second = jnp.where(active, second_next, second_moment)
    new_weights = jnp.where(active, weights_next, weights)
    return (new_weights, new_first, new_second)


def solution(mesh):
    placed = (
        P(("grp", "loc"), None),
        P(("grp", "loc"), None),
        P(("grp", "loc")),
        P(("grp", "loc"), None),
        P(("grp", "loc"), None),
        P(("grp", "loc"), None),
    )
    return jax.shard_map(
        on_device,
        mesh=mesh,
        in_specs=placed,
        out_specs=(P(("grp", "loc"), None), P(("grp", "loc"), None), P(("grp", "loc"), None)),
        check_vma=False,
    )
```

profile of v0, /device:TPU:1, one launch (start us, length us, event | category | flops | bytes accessed | tf_op | source)
XLA Modules:
  0.0 156.7 jit_solution(15181762624817489167)
XLA Ops:
  0.6 1.3 convert_reduce_fusion.1
  1.9 0.7 compare_select_fusion
  2.6 4.5 %scatter_custom_fusion = s32[2304]{0:T(1024)S(1)} fusion(s32[1024]{0:T(1024)S(1)} %bitcast.11, s32[1024]{0:T(1024)} %param.8, s32[]{:T(128)} %constant.12.clone.1), kind=kCustom, calls=%fused_computation.18 | custom fusion | bytes 9728 | tf_op jit(solution)/shard_map/scatter | solution.py:24
  7.3 0.2 copy.19
  7.5 0.7 reshape.44
  8.2 15.7 %all-to-all-start = ((s32[12,1,192]{2,1,0:T(1,128)}), s32[12,1,192]{2,1,0:T(1,128)S(1)}, u32[]{:S(2)}, u32[]{:S(2)}) async-start(s32[12,1,192]{2,1,0:T(1,128)} %reshape.44), calls=%async_computation | async-start | bytes 24576 | tf_op jit(solution)/shard_map/all_to_all | solution.py:29
  23.9 3.8 %scatter_custom_fusion.1 = f32[2304,128]{1,0:T(8,128)S(1)} fusion(s32[1024]{0:T(1024)S(1)} %bitcast.12, f32[1024,128]{1,0:T(8,128)} %param.6, f32[]{:T(128)} %constant.1.clone.1), kind=kCustom, calls=%fused_computation.11 | custom fusion | bytes 1180160 | tf_op jit(solution)/shard_map/scatter | solution.py:23
  27.7 0.5 reshape.22
  28.3 1.4 copy.22
  29.6 3.3 %all-to-all-done = s32[12,1,192]{2,1,0:T(1,128)S(1)} async-done(((s32[12,1,192]{2,1,0:T(1,128)}), s32[12,1,192]{2,1,0:T(1,128)S(1)}, u32[]{:S(2)}, u32[]{:S(2)}) %all-to-all-start) | async-done | bytes 9248 | tf_op jit(solution)/shard_map/all_to_all | solution.py:29
  32.9 5.8 %all-to-all-start.2 = ((f32[64,12,3,128]{3,0,2,1:T(8,128)}), f32[64,12,3,128]{3,0,2,1:T(8,128)S(1)}, u32[]{:S(2)}, u32[]{:S(2)}) async-start(f32[64,12,3,128]{3,0,2,1:T(8,128)} %copy.22), calls=%async_computation.2 | async-start | bytes 2359296 | tf_op jit(solution)/shard_map/all_to_all | solution.py:28
  38.7 0.5 broadcast.18
  39.2 0.7 reduce
  40.0 0.8 copy.20
  40.8 37.1 %all-to-all-done.2 = f32[64,12,3,128]{3,0,2,1:T(8,128)S(1)} async-done(((f32[64,12,3,128]{3,0,2,1:T(8,128)}), f32[64,12,3,128]{3,0,2,1:T(8,128)S(1)}, u32[]{:S(2)}, u32[]{:S(2)}) %all-to-all-start.2) | async-done | bytes 1179680 | tf_op jit(solution)/shard_map/all_to_all | solution.py:28
  77.8 16.6 %all-to-all-start.1 = ((s32[64,12,3]{1,2,0:T(4,128)}), s32[64,12,3]{1,2,0:T(4,128)S(1)}, u32[]{:S(2)}, u32[]{:S(2)}) async-start(s32[64,12,3]{1,2,0:T(4,128)} %copy.20), calls=%async_computation.1 | async-start | bytes 262144 | tf_op jit(solution)/shard_map/all_to_all | solution.py:33
  94.4 2.0 %copy.23 = f32[64,12,3,128]{3,2,1,0:T(4,128)} copy(f32[64,12,3,128]{3,0,2,1:T(8,128)S(1)} %all-to-all-done.2) | data formatting | bytes 2359296 | tf_op jit(solution)/shard_map/all_to_all | solution.py:28
  96.4 9.1 %all-to-all-done.1 = s32[64,12,3]{1,2,0:T(4,128)S(1)} async-done(((s32[64,12,3]{1,2,0:T(4,128)}), s32[64,12,3]{1,2,0:T(4,128)S(1)}, u32[]{:S(2)}, u32[]{:S(2)}) %all-to-all-start.1) | async-done | bytes 9248 | tf_op jit(solution)/shard_map/all_to_all | solution.py:33
  105.5 4.5 %all-to-all-start.3 = ((f32[64,12,3,128]{3,2,1,0:T(4,128)}), f32[64,12,3,128]{3,2,1,0:T(4,128)S(1)}, u32[]{:S(2)}, u32[]{:S(2)}) async-start(f32[64,12,3,128]{3,2,1,0:T(4,128)} %copy.23), calls=%async_computation.3 | async-start | bytes 3145728 | tf_op jit(solution)/shard_map/all_to_all | solution.py:32
  110.1 0.5 copy.21
  110.8 1.0 convert_reduce_fusion
  111.8 37.4 %all-to-all-done.3 = f32[64,12,3,128]{3,2,1,0:T(4,128)S(1)} async-done(((f32[64,12,3,128]{3,2,1,0:T(4,128)}), f32[64,12,3,128]{3,2,1,0:T(4,128)S(1)}, u32[]{:S(2)}, u32[]{:S(2)}) %all-to-all-start.3) | async-done | bytes 1179680 | tf_op jit(solution)/shard_map/all_to_all | solution.py:32
  149.2 0.6 reshape.23
  149.8 6.9 %fusion.7 = (f32[1024,128]{1,0:T(8,128)}, f32[1024,128]{1,0:T(8,128)}, f32[1024,128]{1,0:T(8,128)}) fusion(f32[1024,128]{1,0:T(8,128)S(1)} %copy-done, pred[1024]{0:T(1024)(128)(4,1)S(1)} %broadcast_compare_fusion, f32[1024,128]{1,0:T(8,128)} %param.9, f32[1024,128]{1,0:T(8,128)} %param.10, f32[2304,128]{1,0:T(8,128)S(1)} %reshape.23, s32[2304]{0:T(1024)S(1)} %eq.29), kind=kOutput, calls=%fused_computation.16 | convolution fusion | flops 3628204032 | bytes 4335616 | tf_op jit(solution)/shard_map/dot_general | solution.py:39
  (6 shorter events, 0.5 us)
Async XLA Ops:
  8.2 24.7 %all-to-all-start = ((s32[12,1,192]{2,1,0:T(1,128)}), s32[12,1,192]{2,1,0:T(1,128)S(1)}, u32[]{:S(2)}, u32[]{:S(2)}) async-start(s32[12,1,192]{2,1,0:T(1,128)} %reshape.44), calls=%async_computation | async-start | bytes 24576 | tf_op jit(solution)/shard_map/all_to_all | solution.py:29
  32.9 44.9 %all-to-all-start.2 = ((f32[64,12,3,128]{3,0,2,1:T(8,128)}), f32[64,12,3,128]{3,0,2,1:T(8,128)S(1)}, u32[]{:S(2)}, u32[]{:S(2)}) async-start(f32[64,12,3,128]{3,0,2,1:T(8,128)} %copy.22), calls=%async_computation.2 | async-start | bytes 2359296 | tf_op jit(solution)/shard_map/all_to_all | solution.py:28
  77.8 27.7 %all-to-all-start.1 = ((s32[64,12,3]{1,2,0:T(4,128)}), s32[64,12,3]{1,2,0:T(4,128)S(1)}, u32[]{:S(2)}, u32[]{:S(2)}) async-start(s32[64,12,3]{1,2,0:T(4,128)} %copy.20), calls=%async_computation.1 | async-start | bytes 262144 | tf_op jit(solution)/shard_map/all_to_all | solution.py:33
  105.5 43.6 %all-to-all-start.3 = ((f32[64,12,3,128]{3,2,1,0:T(4,128)}), f32[64,12,3,128]{3,2,1,0:T(4,128)S(1)}, u32[]{:S(2)}, u32[]{:S(2)}) async-start(f32[64,12,3,128]{3,2,1,0:T(4,128)} %copy.23), calls=%async_computation.3 | async-start | bytes 3145728 | tf_op jit(solution)/shard_map/all_to_all | solution.py:32
  110.6 39.2 %copy-start = (f32[1024,128]{1,0:T(8,128)S(1)}, f32[1024,128]{1,0:T(8,128)}, u32[]{:S(2)}) copy-start(f32[1024,128]{1,0:T(8,128)} %param.11) | copy-start | bytes 1572868
where the time goes:
time: 157 us
  waiting for transfers between devices  86.9 us (55%)
  starting transfers between devices  42.6 us (27%)
  local copies, waits for them, and re-layouts  15.9 us (10%)
  matrix products  6.89 us (4%)
  other arithmetic  3.67 us (2%)
    all_to_all x1, waiting for transfers between devices, on_device(): lax.all_to_all(middle[0], 'grp', split_axis=0, concat_axis=0, tiled=True)  37.4 us
    all_to_all x1, waiting for transfers between devices, on_device(): lax.all_to_all(send_grads, 'loc', split_axis=1, concat_axis=1, tiled=True)  37.1 us
    all_to_all x1, starting transfers between devices, on_device(): lax.all_to_all(middle[1], 'grp', split_axis=0, concat_axis=0, tiled=True)  16.6 us
    all_to_all x1, starting transfers between devices, on_device(): lax.all_to_all(send_slots, 'loc', split_axis=1, concat_axis=1, tiled=True)  15.7 us
    all_to_all x1, waiting for transfers between devices, on_device(): lax.all_to_all(middle[1], 'grp', split_axis=0, concat_axis=0, tiled=True)  9.15 us
    dot_general x1, matrix products, on_device(): jnp.dot(selector, got_grads, precision=lax.Precision.HIGHEST, preferred_e...  6.89 us
    all_to_all x1, starting transfers between devices, on_device(): lax.all_to_all(send_grads, 'loc', split_axis=1, concat_axis=1, tiled=True)  5.79 us
    all_to_all x1, starting transfers between devices, on_device(): lax.all_to_all(middle[0], 'grp', split_axis=0, concat_axis=0, tiled=True)  4.51 us
  transfers between devices with their start and end apart: 4, of which 4 were waited for; matrix products, arithmetic and copies ran while one was open for 7% of the time, Pallas kernels for 0%

commit v1 on v0

v1 whole, which is shorter than its diff:
```python
import jax
import jax.numpy as jnp
from jax import lax
from jax.experimental import pallas as pl
from jax.experimental.pallas import tpu as pltpu
from jax.sharding import PartitionSpec as P

STEP = 1000
VMEM = 60 * 1024 * 1024
MESH = pl.DeviceIdType.MESH
F32, BF16, I32 = jnp.float32, jnp.bfloat16, jnp.int32

NY, NXC, NL, CAP = 8, 8, 12, 3
ROWS, WIDTH = 1024, 128
ZROWS = NXC * CAP
SROWS = 40
LANES = NXC * SROWS


def iota(shape, dim):
    return lax.broadcasted_iota(I32, shape, dim)


def onehot(mask):
    return jnp.where(mask, 1.0, 0.0).astype(BF16)


def split(value):
    high = value.astype(BF16)
    low = (value - high.astype(F32)).astype(BF16)
    return jnp.concatenate([high, low], axis=1)


def join(value):
    return value[:, :WIDTH] + value[:, WIDTH:]


def dot(a, b):
    return jnp.dot(a, b, preferred_element_type=F32)


def dot_t(a, b):
    return lax.dot_general(a, b, (((1,), (1,)), ((), ())), preferred_element_type=F32)


def y_distance(chunk):
    hops = (8 - chunk) // 2
    return hops if chunk % 2 else (8 - hops) % 8


def exchange(
    grad_hbm, owner_hbm, slot_hbm, weights_hbm, first_hbm, second_hbm, new_weights, new_first, new_second,
    grad, owner, slot, weights, first, second, parts, zsend, zrecv, zslot_send, zslot_recv, ssend, frecv, wslots, place, acc, count,
    zsem, zrsem, zssem, zsrsem, ssem, frsem, insem,
):
    load = pltpu.make_async_copy(grad_hbm, grad, insem.at[0])
    load.start()
    ids = [
        pltpu.make_async_copy(owner_hbm, owner, insem.at[4]),
        pltpu.make_async_copy(slot_hbm, slot, insem.at[5]),
    ]
    for copy in ids:
        copy.start()
    grp, loc = lax.axis_index("grp"), lax.axis_index("loc")
    my_y, my_xc = grp // NXC, lax.rem(grp, NXC)

    barrier = pltpu.get_barrier_semaphore()
    for step in range(1, NL):
        pl.semaphore_signal(
            barrier, inc=1, device_id=(grp, lax.rem(loc + step, NL)), device_id_type=MESH
        )

    @pl.loop(1, NY * NXC)
    def _(step):
        pl.semaphore_signal(
            barrier, inc=1, device_id=(lax.rem(grp + step, NY * NXC), loc), device_id_type=MESH
        )

    for copy in ids:
        copy.wait()
    own = owner[...]
    group = lax.shift_right_logical(own * 43691, 19)
    index = own - NL * group
    distance = jnp.bitwise_and(lax.shift_right_logical(group, 3) - my_y + NY, NY - 1)
    xc = jnp.bitwise_and(group, NXC - 1)
    hops = jnp.minimum(distance, NY - distance)
    chunk = jnp.maximum(0, 7 - 2 * hops + (distance > 4).astype(I32))

    def rows(tile):
        return jnp.concatenate([tile[b : b + 1, :] for b in range(8)], axis=1)

    own_f = own.astype(F32)
    own_row = rows(own_f)
    own_col = jnp.concatenate([own_f] * 16, axis=0).T
    earlier = iota((128, 128), 0) < iota((128, 128), 1)
    ranks = []
    for ib in range(8):
        mine = own_row[:, ib * 128 : (ib + 1) * 128]
        total = jnp.zeros((128, 128), F32)
        for jb in range(ib + 1):
            same = own_col[:, jb : jb + 1] == mine
            if jb == ib:
                same = jnp.logical_and(same, earlier)
            total = total + jnp.where(same, 1.0, 0.0)
        ranks.append(jnp.sum(total, axis=0, keepdims=True))
    rank = jnp.concatenate(ranks, axis=1).astype(I32)
    chunk_row, index_row, xc_row = rows(chunk), rows(index), rows(xc)
    code = chunk_row * (NL * ZROWS) + index_row * ZROWS + xc_row * CAP + rank

    slot_row = rows(slot[...]) + 1
    line = index_row * NY + chunk_row == iota((NL * NY, ROWS), 0)
    high = lax.shift_right_logical(slot_row, 5).astype(F32)
    low = jnp.bitwise_and(slot_row, 31).astype(F32)
    lines = jnp.concatenate([jnp.where(line, high, 0.0), jnp.where(line, low, 0.0)], axis=0)
    place_lane = onehot(rank * NXC + xc_row == iota((128, ROWS), 0))
    slots = dot_t(lines.astype(BF16), place_lane)
    slots = 32.0 * slots[: NL * NY] + slots[NL * NY :]
    zslot_send[...] = slots.reshape(NL, NY, 128)

    load.wait()
    parts[...] = split(grad[...])

    def z_compute(c):
        pick = onehot(code == iota((NL * ZROWS, ROWS), 0) + c * (NL * ZROWS))
        out = join(dot(pick, parts[...]))
        zsend[c] = out.reshape(NL, ZROWS, WIDTH)
        zrecv[c, loc] = zsend[c, loc]

    z_compute(0)
    zslot_recv[loc] = zslot_send[loc]
    pl.semaphore_wait(barrier, NL - 1 + NY * NXC - 1)

    z_order = (6, 5, 7, 4, 8, 3, 9, 2, 10, 1, 11)
    for step in z_order:
        to = lax.rem(loc + step, NL)
        pltpu.make_async_remote_copy(
            zslot_send.at[to], zslot_recv.at[loc], zssem, zsrsem,
            device_id=(grp, to), device_id_type=MESH,
        ).start()

    def z_send(c):
        for step in z_order:
            to = lax.rem(loc + step, NL)
            pltpu.make_async_remote_copy(
                zsend.at[c, to], zrecv.at[c, loc], zsem.at[c], zrsem.at[c],
                device_id=(grp, to), device_id_type=MESH,
            ).start()

    def wait(block, sem):
        pltpu.make_async_copy(block, block, sem).wait()

    z_send(0)
    for c in range(1, NY):
        z_compute(c)
        z_send(c)

    tables = [
        pltpu.make_async_copy(weights_hbm, weights, insem.at[1]),
        pltpu.make_async_copy(first_hbm, first, insem.at[2]),
        pltpu.make_async_copy(second_hbm, second, insem.at[3]),
    ]
    for table in tables:
        table.start()

    to_row, from_row = iota((LANES, NL * ZROWS), 0), iota((LANES, NL * ZROWS), 1)
    to_xc, to_rest = to_row // SROWS, to_row % SROWS
    wanted = (to_rest // CAP) * ZROWS + to_xc * CAP + to_rest % CAP
    place[...] = onehot(jnp.logical_and(wanted == from_row, to_rest < NL * CAP))
    acc[...] = jnp.zeros_like(acc)
    count[...] = jnp.zeros_like(count)

    wait(zslot_send.at[pl.ds(0, NL - 1)], zsrsem)
    got = jnp.concatenate([zslot_recv[...].reshape(NL * NY, 128), jnp.zeros((32, 128), F32)], axis=0).T
    high = jnp.floor(got * (1.0 / 32.0))
    low = got - 32.0 * high
    lane = iota((128, 384), 1) - my_xc * SROWS
    line = iota((128, 384), 0)
    for c in range(NY):
        total = jnp.zeros((NXC, 384), F32)
        for k in range(CAP):
            part = slice(k * NXC, (k + 1) * NXC)
            both = jnp.concatenate([high[part], low[part]], axis=0).astype(BF16)
            at = onehot(jnp.logical_and(lane == (line // NY) * CAP + k, line % NY == c))
            moved = dot(both, at)
            total = total + 32.0 * moved[:NXC] + moved[NXC:]
        wslots[c] = total

    def s_stage(c):
        wait(zsend.at[c, pl.ds(0, NL - 1)], zrsem.at[c])
        moved = join(dot(place[...], split(zrecv[c].reshape(NL * ZROWS, WIDTH))))
        ssend[c] = moved.reshape(NXC, SROWS, WIDTH)
        for x in range(NXC):
            for t in range(3):
                row = NL * CAP + t
                ssend[c, x, row : row + 1, :] = wslots[c, x : x + 1, t * 128 : (t + 1) * 128]
        away = y_distance(c)
        to_y = lax.rem(my_y + away, NY)
        for step in range(NXC):
            to = lax.rem(my_xc + step, NXC)
            if away == 0 and step == 0:
                frecv[c, my_xc] = ssend[c, my_xc]
                continue
            pltpu.make_async_remote_copy(
                ssend.at[c, to], frecv.at[c, my_xc], ssem.at[c], frsem.at[c],
                device_id=(to_y * NXC + to, loc), device_id_type=MESH,
            ).start()

    def f_stage(c):
        many = NXC - 1 if y_distance(c) == 0 else NXC
        wait(ssend.at[c, pl.ds(0, many)], frsem.at[c])
        got = frecv[c]
        line = jnp.sum(got[:, NL * CAP : NL * CAP + 3, :], axis=0)
        line = jnp.concatenate([line[t : t + 1, :] for t in range(3)], axis=1).astype(I32)
        data = split(got.reshape(LANES, WIDTH))

        @pl.loop(0, 4)
        def _(b):
            at = pl.ds(pl.multiple_of(b * 256, 256), 256)
            hit = jnp.where(line == iota((256, 384), 0) + (b * 256 + 1), 1.0, 0.0)
            acc[at, :] += dot(hit[:, :LANES].astype(BF16), data)
            count[at, :] += hit[:, :128] + hit[:, 128:256] + hit[:, 256:]

    s_stage(0)
    s_stage(1)
    for c in range(2, 7):
        s_stage(c)
        f_stage(c - 2)
    f_stage(5)
    s_stage(7)
    f_stage(6)
    for table in tables:
        table.wait()
    f_stage(7)

    for b in range(4):
        at = pl.ds(b * 256, 256)
        summed = join(acc[at, :])
        active = dot(count[at, :].astype(BF16), jnp.ones((128, WIDTH), BF16)) > 0.5
        old_first, old_second, old_weights = first[at, :], second[at, :], weights[at, :]
        first_next = 0.9 * old_first + 0.1 * summed
        second_next = 0.99 * old_second + 0.01 * summed * summed
        first_hat = first_next / (1.0 - 0.9**STEP)
        second_hat = second_next / (1.0 - 0.99**STEP)
        weights_next = old_weights - 0.5 * first_hat / (jnp.sqrt(second_hat) + 1e-08)
        new_first[at, :] = jnp.where(active, first_next, old_first)
        new_second[at, :] = jnp.where(active, second_next, old_second)
        new_weights[at, :] = jnp.where(active, weights_next, old_weights)

    wait(zslot_send.at[pl.ds(0, NL - 1)], zssem)
    for c in range(NY):
        wait(zsend.at[c, pl.ds(0, NL - 1)], zsem.at[c])
        many = NXC - 1 if y_distance(c) == 0 else NXC
        wait(ssend.at[c, pl.ds(0, many)], ssem.at[c])


def store(weights, first, second, weights_hbm, first_hbm, second_hbm, sems):
    pairs = ((weights, weights_hbm), (first, first_hbm), (second, second_hbm))
    copies = [pltpu.make_async_copy(a, b, sems.at[i]) for i, (a, b) in enumerate(pairs)]
    for copy in copies:
        copy.start()
    for copy in copies:
        copy.wait()


def on_device(grad_rows, row_owner, row_slot, weights, first_moment, second_moment):
    vmem = pl.BlockSpec(memory_space=pltpu.VMEM)
    dma = pltpu.SemaphoreType.DMA
    hbm = pl.BlockSpec(memory_space=pltpu.HBM)
    out = jax.ShapeDtypeStruct((ROWS, WIDTH), F32)
    results = pl.pallas_call(
        exchange,
        out_shape=(out, out, out),
        in_specs=[hbm] * 6,
        out_specs=(vmem, vmem, vmem),
        scratch_shapes=[
            pltpu.VMEM((ROWS, WIDTH), F32),
            pltpu.VMEM((8, 128), I32),
            pltpu.VMEM((8, 128), I32),
            pltpu.VMEM((ROWS, WIDTH), F32),
            pltpu.VMEM((ROWS, WIDTH), F32),
            pltpu.VMEM((ROWS, WIDTH), F32),
            pltpu.VMEM((ROWS, 2 * WIDTH), BF16),
            pltpu.VMEM((NY, NL, ZROWS, WIDTH), F32),
            pltpu.VMEM((NY, NL, ZROWS, WIDTH), F32),
            pltpu.VMEM((NL, NY, 128), F32),
            pltpu.VMEM((NL, NY, 128), F32),
            pltpu.VMEM((NY, NXC, SROWS, WIDTH), F32),
            pltpu.VMEM((NY, NXC, SROWS, WIDTH), F32),
            pltpu.VMEM((NY, NXC, 384), F32),
            pltpu.VMEM((LANES, NL * ZROWS), BF16),
            pltpu.VMEM((ROWS, 2 * WIDTH), F32),
            pltpu.VMEM((ROWS, 128), F32),
            dma((NY,)),
            dma((NY,)),
            dma,
            dma,
            dma((NY,)),
            dma((NY,)),
            dma((6,)),
        ],
        compiler_params=pltpu.CompilerParams(
            collective_id=0, has_side_effects=True, vmem_limit_bytes=VMEM
        ),
        name="exchange",
    )(
        grad_rows, row_owner.reshape(8, 128), row_slot.reshape(8, 128),
        weights, first_moment, second_moment,
    )
    return pl.pallas_call(
        store,
        out_shape=(out, out, out),
        in_specs=[vmem] * 3,
        out_specs=(hbm, hbm, hbm),
        scratch_shapes=[dma((3,))],
        compiler_params=pltpu.CompilerParams(vmem_limit_bytes=VMEM),
        name="store",
    )(*results)


def solution(mesh):
    placed = (
        P(("grp", "loc"), None),
        P(("grp", "loc"), None),
        P(("grp", "loc")),
        P(("grp", "loc"), None),
        P(("grp", "loc"), None),
        P(("grp", "loc"), None),
    )
    return jax.shard_map(
        on_device,
        mesh=mesh,
        in_specs=placed,
        out_specs=(P(("grp", "loc"), None), P(("grp", "loc"), None), P(("grp", "loc"), None)),
        check_vma=False,
    )
```

time: 157 us -> 75.6 us (0.48)
  waiting for transfers between devices: 86.9 us -> 0 us
  Pallas kernels: 0 us -> 74.8 us
  starting transfers between devices: 42.6 us -> 0 us
  local copies, waits for them, and re-layouts: 15.9 us -> 0 us
  matrix products: 6.89 us -> 0 us
  other arithmetic: 3.67 us -> 0 us
    all_to_all x4 -> x0, waiting for transfers between devices: 86.9 us -> none  [the longest x1 37.4 us: on_device(): lax.all_to_all(middle[0], 'grp', split_axis=0, concat_axis=0, tiled=True)]
    pallas_call x0 -> x2, Pallas kernels: none -> 74.8 us  [the longest x1 72.3 us: on_device(): pl.pallas_call(exchange, out_shape=(out, out, out), in_specs=[hbm] * 6, o...]
    all_to_all x4 -> x0, starting transfers between devices: 42.6 us -> none  [the longest x1 16.6 us: on_device(): lax.all_to_all(middle[1], 'grp', split_axis=0, concat_axis=0, tiled=True)]
    scatter x2 -> x0, local copies, waits for them, and re-layouts: 8.26 us -> none  [the longest x1 4.49 us: on_device(): jnp.full((devices_all * capacity,), -1, jnp.int32).at[position]]
    dot_general x1 -> x0, matrix products: 6.89 us -> none  [on_device(): jnp.dot(selector, got_grads, precision=lax.Precision.HIGHEST, preferred_e...]
    all_to_all x4 -> x0, local copies, waits for them, and re-layouts: 3.76 us -> none  [the longest x1 1.96 us: on_device(): lax.all_to_all(send_grads, 'loc', split_axis=1, concat_axis=1, tiled=True)]
    reshape x5 -> x0, local copies, waits for them, and re-layouts: 2.91 us -> none  [the longest x2 1.92 us: on_device(): send_grads = send_grads.reshape(group_count, local_count, capacity, width)]
    reduce_sum x2 -> x0, other arithmetic: 2.29 us -> none  [the longest x1 1.28 us: on_device(): jnp.sum(jnp.logical_and(same_owner, before).astype(jnp.int32), axis=1)]
  transfers between devices with their start and end apart: 4 -> 0, of which waited for: 4 -> 0; matrix products, arithmetic and copies ran while one was open for 7% -> 0% of each run, Pallas kernels for 0% -> 0%
where the time goes in v1:
time: 75.6 us; the launch traced here: 75.5 us
  Pallas kernels  74.8 us (99%)
    pallas_call x1, Pallas kernels, on_device(): pl.pallas_call(exchange, out_shape=(out, out, out), in_specs=[hbm] * 6, o...  72.3 us
    pallas_call x1, Pallas kernels, on_device(): pl.pallas_call(store, out_shape=(out, out, out), in_specs=[vmem] * 3, out...  2.52 us

profile of v1, /device:TPU:1, one launch (start us, length us, event | category | flops | bytes accessed | tf_op | source)
XLA Modules:
  0.0 75.5 jit_solution(17350800869386488044)
XLA Ops:
  0.6 72.3 %exchange.1 = (f32[1024,128]{1,0:T(8,128)}, f32[1024,128]{1,0:T(8,128)}, f32[1024,128]{1,0:T(8,128)}) custom-call(f32[1024,128]{1,0:T(8,128)} %grad_hbm.1, s32[8,128]{1,0:T(8,128)} %bitcast.2, s32[8,128]{1,0:T(8,128)} %bitcast.3, f32[1024,128]{1,0:T(8,128)} %weights_hbm.1, f32[1024,128]{1,0:T(8,128)} %first_hbm.1, f32[1024,128]{1,0:T(8,128)} %second_hbm.1), custom_call_target="tpu_custom_call" | custom-call | tf_op jit(solution)/shard_map/exchange/pallas_call | solution.py:270
  73.0 2.5 %store.1 = (f32[1024,128]{1,0:T(8,128)}, f32[1024,128]{1,0:T(8,128)}, f32[1024,128]{1,0:T(8,128)}) custom-call(f32[1024,128]{1,0:T(8,128)} %get-tuple-element.6.weights, f32[1024,128]{1,0:T(8,128)} %get-tuple-element.7.first, f32[1024,128]{1,0:T(8,128)} %get-tuple-element.8.second), custom_call_target="tpu_custom_call" | custom-call | tf_op jit(solution)/shard_map/store/pallas_call | solution.py:309

commit v2 on v1

--- a/solution.py
+++ b/solution.py
@@ -12,9 +12,11 @@
 
 NY, NXC, NL, CAP = 8, 8, 12, 3
 ROWS, WIDTH = 1024, 128
-ZROWS = NXC * CAP
 SROWS = 40
 LANES = NXC * SROWS
+GROUPS = (((0,), 24), ((1, 2), 40), ((3, 4), 40), ((5, 6, 7), 48))
+GROUP_OF = (0, 1, 1, 2, 2, 3, 3, 3)
+FLAG = 127
 
 
 def iota(shape, dim):
@@ -49,8 +51,9 @@
 
 
 def exchange(
-    grad_hbm, owner_hbm, slot_hbm, weights_hbm, first_hbm, second_hbm, new_weights, new_first, new_second,
-    grad, owner, slot, weights, first, second, parts, zsend, zrecv, zslot_send, zslot_recv, ssend, frecv, wslots, place, acc, count,
+    grad_hbm, owner_hbm, slot_hbm, weights_hbm, first_hbm, second_hbm, new_weights, new_first, new_second, over,
+    grad, owner, slot, weights, first, second, parts, zsend0, zsend1, zsend2, zsend3,
+    zrecv0, zrecv1, zrecv2, zrecv3, zslot_send, zslot_recv, ssend, frecv, wslots, place, acc, count,
     zsem, zrsem, zssem, zsrsem, ssem, frsem, insem,
 ):
     load = pltpu.make_async_copy(grad_hbm, grad, insem.at[0])
@@ -63,6 +66,7 @@
         copy.start()
     grp, loc = lax.axis_index("grp"), lax.axis_index("loc")
     my_y, my_xc = grp // NXC, lax.rem(grp, NXC)
+    zsend, zrecv = (zsend0, zsend1, zsend2, zsend3), (zrecv0, zrecv1, zrecv2, zrecv3)
 
     barrier = pltpu.get_barrier_semaphore()
     for step in range(1, NL):
@@ -89,23 +93,32 @@
     def rows(tile):
         return jnp.concatenate([tile[b : b + 1, :] for b in range(8)], axis=1)
 
-    own_f = own.astype(F32)
-    own_row = rows(own_f)
-    own_col = jnp.concatenate([own_f] * 16, axis=0).T
+    group_of = (chunk >= 1).astype(I32) + (chunk >= 3).astype(I32) + (chunk >= 5).astype(I32)
     earlier = iota((128, 128), 0) < iota((128, 128), 1)
-    ranks = []
-    for ib in range(8):
-        mine = own_row[:, ib * 128 : (ib + 1) * 128]
-        total = jnp.zeros((128, 128), F32)
-        for jb in range(ib + 1):
-            same = own_col[:, jb : jb + 1] == mine
-            if jb == ib:
-                same = jnp.logical_and(same, earlier)
-            total = total + jnp.where(same, 1.0, 0.0)
-        ranks.append(jnp.sum(total, axis=0, keepdims=True))
-    rank = jnp.concatenate(ranks, axis=1).astype(I32)
-    chunk_row, index_row, xc_row = rows(chunk), rows(index), rows(xc)
-    code = chunk_row * (NL * ZROWS) + index_row * ZROWS + xc_row * CAP + rank
+
+    def rank_of(key):
+        key_row = rows(key)
+        key_col = jnp.concatenate([key] * 16, axis=0).T
+        ranks = []
+        for ib in range(8):
+            mine = key_row[:, ib * 128 : (ib + 1) * 128]
+            total = jnp.zeros((128, 128), F32)
+            for jb in range(ib + 1):
+                same = key_col[:, jb : jb + 1] == mine
+                if jb == ib:
+                    same = jnp.logical_and(same, earlier)
+                total = total + jnp.where(same, 1.0, 0.0)
+            ranks.append(jnp.sum(total, axis=0, keepdims=True))
+        return jnp.concatenate(ranks, axis=1).astype(I32)
+
+    rank = rank_of(own.astype(F32))
+    zrank = rank_of((index * 4 + group_of).astype(F32))
+    chunk_row, index_row, xc_row, group_row = rows(chunk), rows(index), rows(xc), rows(group_of)
+    room = jnp.full((1, ROWS), GROUPS[0][1], I32)
+    for q in range(1, len(GROUPS)):
+        room = jnp.where(group_row == q, GROUPS[q][1], room)
+    too_many = jnp.max(jnp.where(zrank >= room, 1.0, 0.0), axis=1, keepdims=True)
+    code = jnp.where(zrank < room, index_row * room + zrank, -1)
 
     slot_row = rows(slot[...]) + 1
     line = index_row * NY + chunk_row == iota((NL * NY, ROWS), 0)
@@ -115,16 +128,22 @@
     place_lane = onehot(rank * NXC + xc_row == iota((128, ROWS), 0))
     slots = dot_t(lines.astype(BF16), place_lane)
     slots = 32.0 * slots[: NL * NY] + slots[NL * NY :]
+    spot = jnp.where(line, jnp.minimum(zrank, 127).astype(F32) + 1.0, 0.0).astype(BF16)
+    spot_lane = onehot(rank * NXC + xc_row + 64 == iota((128, ROWS), 0))
+    slots = slots + dot_t(spot, spot_lane)
+    slots = jnp.where(iota((NL * NY, 128), 1) == FLAG, too_many, slots)
     zslot_send[...] = slots.reshape(NL, NY, 128)
 
     load.wait()
     parts[...] = split(grad[...])
 
-    def z_compute(c):
-        pick = onehot(code == iota((NL * ZROWS, ROWS), 0) + c * (NL * ZROWS))
+    def z_compute(q):
+        many = NL * GROUPS[q][1]
+        here = jnp.where(group_row == q, code, -1)
+        pick = onehot(here == iota((many, ROWS), 0))
         out = join(dot(pick, parts[...]))
-        zsend[c] = out.reshape(NL, ZROWS, WIDTH)
-        zrecv[c, loc] = zsend[c, loc]
+        zsend[q][...] = out.reshape(NL, GROUPS[q][1], WIDTH)
+        zrecv[q][loc] = zsend[q][loc]
 
     z_compute(0)
     zslot_recv[loc] = zslot_send[loc]
@@ -138,11 +157,11 @@
             device_id=(grp, to), device_id_type=MESH,
         ).start()
 
-    def z_send(c):
+    def z_send(q):
         for step in z_order:
             to = lax.rem(loc + step, NL)
             pltpu.make_async_remote_copy(
-                zsend.at[c, to], zrecv.at[c, loc], zsem.at[c], zrsem.at[c],
+                zsend[q].at[to], zrecv[q].at[loc], zsem.at[q], zrsem.at[q],
                 device_id=(grp, to), device_id_type=MESH,
             ).start()
 
@@ -150,9 +169,9 @@
         pltpu.make_async_copy(block, block, sem).wait()
 
     z_send(0)
-    for c in range(1, NY):
-        z_compute(c)
-        z_send(c)
+    for q in range(1, len(GROUPS)):
+        z_compute(q)
+        z_send(q)
 
     tables = [
         pltpu.make_async_copy(weights_hbm, weights, insem.at[1]),
@@ -162,20 +181,18 @@
     for table in tables:
         table.start()
 
-    to_row, from_row = iota((LANES, NL * ZROWS), 0), iota((LANES, NL * ZROWS), 1)
-    to_xc, to_rest = to_row // SROWS, to_row % SROWS
-    wanted = (to_rest // CAP) * ZROWS + to_xc * CAP + to_rest % CAP
-    place[...] = onehot(jnp.logical_and(wanted == from_row, to_rest < NL * CAP))
     acc[...] = jnp.zeros_like(acc)
     count[...] = jnp.zeros_like(count)
+    over[...] = jnp.zeros_like(over)
 
     wait(zslot_send.at[pl.ds(0, NL - 1)], zsrsem)
     got = jnp.concatenate([zslot_recv[...].reshape(NL * NY, 128), jnp.zeros((32, 128), F32)], axis=0).T
     high = jnp.floor(got * (1.0 / 32.0))
     low = got - 32.0 * high
+    flagged = jnp.sum(got[FLAG : FLAG + 1, :], axis=1, keepdims=True)
     lane = iota((128, 384), 1) - my_xc * SROWS
     line = iota((128, 384), 0)
-    for c in range(NY):
+    def prepare(c):
         total = jnp.zeros((NXC, 384), F32)
         for k in range(CAP):
             part = slice(k * NXC, (k + 1) * NXC)
@@ -183,27 +200,46 @@
             at = onehot(jnp.logical_and(lane == (line // NY) * CAP + k, line % NY == c))
             moved = dot(both, at)
             total = total + 32.0 * moved[:NXC] + moved[NXC:]
-        wslots[c] = total
+        wslots[c] = jnp.where(iota((NXC, 384), 1) == 256 + FLAG, flagged, total)
+
+        spots = jnp.zeros((NXC, 128), F32)
+        for k in range(CAP):
+            part = slice(64 + k * NXC, 64 + (k + 1) * NXC)
+            from_line, to_lane = iota((128, 128), 0), iota((128, 128), 1)
+            at = jnp.logical_and(to_lane == (from_line // NY) * CAP + k, from_line % NY == c)
+            spots = spots + dot(got[part].astype(BF16), onehot(at))
+        spots = jnp.concatenate([spots, jnp.zeros((120, 128), F32)], axis=0).T
+        size = GROUPS[GROUP_OF[c]][1]
+        column = jnp.concatenate([spots[:SROWS, x : x + 1] for x in range(NXC)], axis=0).astype(I32)
+        source = (iota((LANES, 1), 0) % SROWS) // CAP
+        column = jnp.where(column > 0, source * size + column - 1, -1)
+        place[c, :, : NL * size] = onehot(column == iota((LANES, NL * size), 1))
 
     def s_stage(c):
-        wait(zsend.at[c, pl.ds(0, NL - 1)], zrsem.at[c])
-        moved = join(dot(place[...], split(zrecv[c].reshape(NL * ZROWS, WIDTH))))
+        q = GROUP_OF[c]
+        many = NL * GROUPS[q][1]
+        if c == GROUPS[q][0][0]:
+            wait(zsend[q].at[pl.ds(0, NL - 1)], zrsem.at[q])
+        moved = join(dot(place[c, :, :many], split(zrecv[q][...].reshape(many, WIDTH))))
         ssend[c] = moved.reshape(NXC, SROWS, WIDTH)
         for x in range(NXC):
             for t in range(3):
                 row = NL * CAP + t
                 ssend[c, x, row : row + 1, :] = wslots[c, x : x + 1, t * 128 : (t + 1) * 128]
-        away = y_distance(c)
-        to_y = lax.rem(my_y + away, NY)
+
+    def s_send(chunks):
         for step in range(NXC):
             to = lax.rem(my_xc + step, NXC)
-            if away == 0 and step == 0:
-                frecv[c, my_xc] = ssend[c, my_xc]
-                continue
-            pltpu.make_async_remote_copy(
-                ssend.at[c, to], frecv.at[c, my_xc], ssem.at[c], frsem.at[c],
-                device_id=(to_y * NXC + to, loc), device_id_type=MESH,
-            ).start()
+            for c in chunks:
+                away = y_distance(c)
+                if away == 0 and step == 0:
+                    frecv[c, my_xc] = ssend[c, my_xc]
+                    continue
+                to_y = lax.rem(my_y + away, NY)
+                pltpu.make_async_remote_copy(
+                    ssend.at[c, to], frecv.at[c, my_xc], ssem.at[c], frsem.at[c],
+                    device_id=(to_y * NXC + to, loc), device_id_type=MESH,
+                ).start()
 
     def f_stage(c):
         many = NXC - 1 if y_distance(c) == 0 else NXC
@@ -212,6 +248,7 @@
         line = jnp.sum(got[:, NL * CAP : NL * CAP + 3, :], axis=0)
         line = jnp.concatenate([line[t : t + 1, :] for t in range(3)], axis=1).astype(I32)
         data = split(got.reshape(LANES, WIDTH))
+        over[...] += line[:, 256:]
 
         @pl.loop(0, 4)
         def _(b):
@@ -220,17 +257,20 @@
             acc[at, :] += dot(hit[:, :LANES].astype(BF16), data)
             count[at, :] += hit[:, :128] + hit[:, 128:256] + hit[:, 256:]
 
-    s_stage(0)
-    s_stage(1)
-    for c in range(2, 7):
-        s_stage(c)
-        f_stage(c - 2)
-    f_stage(5)
-    s_stage(7)
-    f_stage(6)
+    def s_group(q):
+        for c in GROUPS[q][0]:
+            prepare(c)
+        for c in GROUPS[q][0]:
+            s_stage(c)
+        s_send(GROUPS[q][0])
+
+    for q in range(len(GROUPS)):
+        s_group(q)
+    for c in (0, 1, 2, 3, 4, 7, 5):
+        f_stage(c)
     for table in tables:
         table.wait()
-    f_stage(7)
+    f_stage(6)
 
     for b in range(4):
         at = pl.ds(b * 256, 256)
@@ -247,8 +287,9 @@
         new_weights[at, :] = jnp.where(active, weights_next, old_weights)
 
     wait(zslot_send.at[pl.ds(0, NL - 1)], zssem)
+    for q in range(len(GROUPS)):
+        wait(zsend[q].at[pl.ds(0, NL - 1)], zsem.at[q])
     for c in range(NY):
-        wait(zsend.at[c, pl.ds(0, NL - 1)], zsem.at[c])
         many = NXC - 1 if y_distance(c) == 0 else NXC
         wait(ssend.at[c, pl.ds(0, many)], ssem.at[c])
 
@@ -262,16 +303,62 @@
         copy.wait()
 
 
+def padded(grad_rows, row_owner, row_slot, weights, first_moment, second_moment):
+    group_count = lax.axis_size("grp")
+    local_count = lax.axis_size("loc")
+    devices_all = group_count * local_count
+    rows, width = grad_rows.shape
+    shard = weights.shape[0]
+    capacity = max(2, (2 * rows + devices_all - 1) // devices_all)
+    owner = row_owner[:, 0]
+    same_owner = owner[:, None] == owner[None, :]
+    before = lax.broadcasted_iota(jnp.int32, (rows, rows), 1) < lax.broadcasted_iota(
+        jnp.int32, (rows, rows), 0
+    )
+    rank = jnp.sum(jnp.logical_and(same_owner, before).astype(jnp.int32), axis=1)
+    position = owner * capacity + rank
+    send_grads = jnp.zeros((devices_all * capacity, width), jnp.float32).at[position].set(grad_rows)
+    send_slots = jnp.full((devices_all * capacity,), -1, jnp.int32).at[position].set(row_slot)
+    send_grads = send_grads.reshape(group_count, local_count, capacity, width)
+    send_slots = send_slots.reshape(group_count, local_count, capacity)
+    middle = (
+        lax.all_to_all(send_grads, "loc", split_axis=1, concat_axis=1, tiled=True),
+        lax.all_to_all(send_slots, "loc", split_axis=1, concat_axis=1, tiled=True),
+    )
+    arrived = (
+        lax.all_to_all(middle[0], "grp", split_axis=0, concat_axis=0, tiled=True),
+        lax.all_to_all(middle[1], "grp", split_axis=0, concat_axis=0, tiled=True),
+    )
+    got_grads = arrived[0].reshape(devices_all * capacity, width)
+    got_slots = arrived[1].reshape(devices_all * capacity)
+    table_index = lax.broadcasted_iota(jnp.int32, (shard, devices_all * capacity), 0)
+    selector = (table_index == got_slots[None, :]).astype(jnp.float32)
+    summed = jnp.dot(
+        selector, got_grads, precision=lax.Precision.HIGHEST, preferred_element_type=jnp.float32
+    )
+    touched = jnp.sum(selector, axis=1)
+    active = (touched > 0.5)[:, None]
+    first_next = 0.9 * first_moment + 0.1 * summed
+    second_next = 0.99 * second_moment + 0.01 * summed * summed
+    first_hat = first_next / (1.0 - 0.9**STEP)
+    second_hat = second_next / (1.0 - 0.99**STEP)
+    weights_next = weights - 0.5 * first_hat / (jnp.sqrt(second_hat) + 1e-08)
+    new_first = jnp.where(active, first_next, first_moment)
+    new_second = jnp.where(active, second_next, second_moment)
+    new_weights = jnp.where(active, weights_next, weights)
+    return (new_weights, new_first, new_second)
+
+
 def on_device(grad_rows, row_owner, row_slot, weights, first_moment, second_moment):
     vmem = pl.BlockSpec(memory_space=pltpu.VMEM)
     dma = pltpu.SemaphoreType.DMA
     hbm = pl.BlockSpec(memory_space=pltpu.HBM)
     out = jax.ShapeDtypeStruct((ROWS, WIDTH), F32)
-    results = pl.pallas_call(
+    *results, over = pl.pallas_call(
         exchange,
-        out_shape=(out, out, out),
+        out_shape=(out, out, out, jax.ShapeDtypeStruct((1, 128), I32)),
         in_specs=[hbm] * 6,
-        out_specs=(vmem, vmem, vmem),
+        out_specs=(vmem, vmem, vmem, vmem),
         scratch_shapes=[
             pltpu.VMEM((ROWS, WIDTH), F32),
             pltpu.VMEM((8, 128), I32),
@@ -280,18 +367,18 @@
             pltpu.VMEM((ROWS, WIDTH), F32),
             pltpu.VMEM((ROWS, WIDTH), F32),
             pltpu.VMEM((ROWS, 2 * WIDTH), BF16),
-            pltpu.VMEM((NY, NL, ZROWS, WIDTH), F32),
-            pltpu.VMEM((NY, NL, ZROWS, WIDTH), F32),
+            *[pltpu.VMEM((NL, room, WIDTH), F32) for _, room in GROUPS],
+            *[pltpu.VMEM((NL, room, WIDTH), F32) for _, room in GROUPS],
             pltpu.VMEM((NL, NY, 128), F32),
             pltpu.VMEM((NL, NY, 128), F32),
             pltpu.VMEM((NY, NXC, SROWS, WIDTH), F32),
             pltpu.VMEM((NY, NXC, SROWS, WIDTH), F32),
             pltpu.VMEM((NY, NXC, 384), F32),
-            pltpu.VMEM((LANES, NL * ZROWS), BF16),
+            pltpu.VMEM((NY, LANES, 640), BF16),
             pltpu.VMEM((ROWS, 2 * WIDTH), F32),
             pltpu.VMEM((ROWS, 128), F32),
-            dma((NY,)),
-            dma((NY,)),
+            dma((len(GROUPS),)),
+            dma((len(GROUPS),)),
             dma,
             dma,
             dma((NY,)),
@@ -306,15 +393,21 @@
         grad_rows, row_owner.reshape(8, 128), row_slot.reshape(8, 128),
         weights, first_moment, second_moment,
     )
-    return pl.pallas_call(
-        store,
-        out_shape=(out, out, out),
-        in_specs=[vmem] * 3,
-        out_specs=(hbm, hbm, hbm),
-        scratch_shapes=[dma((3,))],
-        compiler_params=pltpu.CompilerParams(vmem_limit_bytes=VMEM),
-        name="store",
-    )(*results)
+    def packed():
+        return pl.pallas_call(
+            store,
+            out_shape=(out, out, out),
+            in_specs=[vmem] * 3,
+            out_specs=(hbm, hbm, hbm),
+            scratch_shapes=[dma((3,))],
+            compiler_params=pltpu.CompilerParams(vmem_limit_bytes=VMEM),
+            name="store",
+        )(*results)
+
+    def full():
+        return tuple(padded(grad_rows, row_owner, row_slot, weights, first_moment, second_moment))
+
+    return lax.cond(over[0, FLAG] > 0, full, packed)
 
 
 def solution(mesh):

time: 75.6 us -> 73.3 us (0.970)
  Pallas kernels: 74.8 us -> 70.2 us
  local copies, waits for them, and re-layouts: 0 us -> 1.26 us
  between operations: 0.64 us -> 1.5 us
    pallas_call x2, Pallas kernels: 74.8 us -> 70.2 us  [the longest x1 69 us: on_device(): pl.pallas_call(exchange, out_shape=(out, out, out, jax.ShapeDtypeStruct((...]
    slice x0 -> x1, local copies, waits for them, and re-layouts: none -> 1.25 us  [on_device(): return lax.cond(over[0, FLAG] > 0, full, packed)]
where the time goes in v2:
time: 73.3 us; the launch traced here: 73.2 us
  Pallas kernels  70.2 us (96%)
  between operations  1.5 us (2%)
  local copies, waits for them, and re-layouts  1.26 us (2%)
    pallas_call x1, Pallas kernels, on_device(): pl.pallas_call(exchange, out_shape=(out, out, out, jax.ShapeDtypeStruct((...  69 us

profile of v2, /device:TPU:1, one launch (start us, length us, event | category | flops | bytes accessed | tf_op | source)
XLA Modules:
  0.0 73.2 jit_solution(3153381347831381448)
XLA Ops:
  0.6 0.0 copy-start
  0.6 0.0 copy-start.1
  0.7 69.0 %exchange.1 = (f32[1024,128]{1,0:T(8,128)S(1)}, f32[1024,128]{1,0:T(8,128)S(1)}, f32[1024,128]{1,0:T(8,128)S(1)}, s32[1,128]{1,0:T(1,128)}) custom-call(f32[1024,128]{1,0:T(8,128)} %grad_hbm.1, s32[8,128]{1,0:T(8,128)} %bitcast.13, s32[8,128]{1,0:T(8,128)} %bitcast.15, f32[1024,128]{1,0:T(8,128)} %weights_hbm.1, f32[1024,128]{1,0:T(8,128)} %first_hbm.1, ...), custom_call_target="tpu_custom_call" | custom-call | tf_op jit(solution)/shard_map/exchange/pallas_call | solution.py:357
  69.6 1.2 %slice.3 = s32[1,1]{1,0:T(1,128)} slice(s32[1,128]{1,0:T(1,128)} %get-tuple-element.34), slice={[0:1], [127:128]} | slice | bytes 8 | tf_op jit(solution)/shard_map/slice | solution.py:410
  71.5 0.0 copy-done
  71.6 0.0 copy-done.1
  71.6 1.4 %conditional.1 = ((f32[1024,128]{1,0:T(8,128)}, f32[1024,128]{1,0:T(8,128)}, f32[1024,128]{1,0:T(8,128)})) conditional(s32[]{:T(128)} %bitcast.5, (f32[1024,128]{1,0:T(8,128)S(1)}, f32[1024,128]{1,0:T(8,128)S(1)}, f32[1024,128]{1,0:T(8,128)S(1)}) %tuple.14, (s32[1024,1]{0,1:T(1,128)S(1)}, s32[1024]{0:T(1024)}, f32[1024,128]{1,0:T(8,128)}, ...), branch_computations={%region_0.0_spmd, %region_1.6_spmd} | conditional | flops 3640528896 | bytes 23318700 | solution.py:410
  71.6 1.2 %store.1 = (f32[1024,128]{1,0:T(8,128)}, f32[1024,128]{1,0:T(8,128)}, f32[1024,128]{1,0:T(8,128)}) custom-call(f32[1024,128]{1,0:T(8,128)S(1)} %get-tuple-element.18.weights, f32[1024,128]{1,0:T(8,128)S(1)} %get-tuple-element.19.first, f32[1024,128]{1,0:T(8,128)S(1)} %get-tuple-element.20.second), custom_call_target="tpu_custom_call" | custom-call | tf_op jit(solution)/shard_map/cond/branch_0_fun/store/pallas_call | solution.py:397
Async XLA Ops:
  0.6 70.9 %copy-start = (f32[1024,128]{1,0:T(8,128)S(1)}, f32[1024,128]{1,0:T(8,128)}, u32[]{:S(2)}) copy-start(f32[1024,128]{1,0:T(8,128)} %weights_hbm.1) | copy-start | bytes 1572868
  0.6 70.9 %copy-start.1 = (s32[1024,1]{0,1:T(1,128)S(1)}, s32[1024,1]{0,1:T(1,128)}, u32[]{:S(2)}) copy-start(s32[1024,1]{0,1:T(1,128)} %param.9) | copy-start | bytes 12292

commit v3 on v2

--- a/solution.py
+++ b/solution.py
@@ -248,7 +248,7 @@
         line = jnp.sum(got[:, NL * CAP : NL * CAP + 3, :], axis=0)
         line = jnp.concatenate([line[t : t + 1, :] for t in range(3)], axis=1).astype(I32)
         data = split(got.reshape(LANES, WIDTH))
-        over[...] += line[:, 256:]
+        over[...] += jnp.where(iota((1, 128), 1) == FLAG, line[:, 256:], 0)
 
         @pl.loop(0, 4)
         def _(b):
@@ -407,7 +407,7 @@
     def full():
         return tuple(padded(grad_rows, row_owner, row_slot, weights, first_moment, second_moment))
 
-    return lax.cond(over[0, FLAG] > 0, full, packed)
+    return lax.cond(jnp.max(over) > 0, full, packed)
 
 
 def solution(mesh):

time: 73.3 us -> 73.3 us (level)
  other arithmetic: 0 us -> 1.32 us
  local copies, waits for them, and re-layouts: 1.26 us -> 0.01 us
    reduce_max x0 -> x1, other arithmetic: none -> 1.32 us  [on_device(): return lax.cond(jnp.max(over) > 0, full, packed)]
    slice x1 -> x0, local copies, waits for them, and re-layouts: 1.25 us -> none  [on_device(): return lax.cond(over[0, FLAG] > 0, full, packed)]
where the time goes in v3:
time: 73.3 us; the launch traced here: 73.2 us
  Pallas kernels  70.1 us (96%)
  between operations  1.5 us (2%)
  other arithmetic  1.32 us (2%)
    pallas_call x1, Pallas kernels, on_device(): pl.pallas_call(exchange, out_shape=(out, out, out, jax.ShapeDtypeStruct((...  69 us

profile of v3, /device:TPU:1, one launch (start us, length us, event | category | flops | bytes accessed | tf_op | source)
XLA Modules:
  0.0 73.2 jit_solution(8330737223192049749)
XLA Ops:
  0.6 0.0 copy-start
  0.6 0.0 copy-start.1
  0.7 69.0 %exchange.1 = (f32[1024,128]{1,0:T(8,128)S(1)}, f32[1024,128]{1,0:T(8,128)S(1)}, f32[1024,128]{1,0:T(8,128)S(1)}, s32[1,128]{1,0:T(1,128)}) custom-call(f32[1024,128]{1,0:T(8,128)} %grad_hbm.1, s32[8,128]{1,0:T(8,128)} %bitcast.12, s32[8,128]{1,0:T(8,128)} %bitcast.14, f32[1024,128]{1,0:T(8,128)} %weights_hbm.1, f32[1024,128]{1,0:T(8,128)} %first_hbm.1, ...), custom_call_target="tpu_custom_call" | custom-call | tf_op jit(solution)/shard_map/exchange/pallas_call | solution.py:357
  69.6 1.3 %reduce_max.9 = s32[]{:T(128)} reduce(s32[1,128]{1,0:T(1,128)} %get-tuple-element.34, s32[]{:T(128)} %constant.9.clone.1), dimensions={0,1}, to_apply=%region_0.0 | reduce | flops 127 | bytes 520 | tf_op jit(solution)/shard_map/reduce_max | solution.py:410
  71.6 0.0 copy-done
  71.6 0.0 copy-done.1
  71.6 1.4 %conditional.1 = ((f32[1024,128]{1,0:T(8,128)}, f32[1024,128]{1,0:T(8,128)}, f32[1024,128]{1,0:T(8,128)})) conditional(s32[]{:T(128)} %convert_element_type.9, (f32[1024,128]{1,0:T(8,128)S(1)}, f32[1024,128]{1,0:T(8,128)S(1)}, f32[1024,128]{1,0:T(8,128)S(1)}) %tuple.14, (s32[1024,1]{0,1:T(1,128)S(1)}, s32[1024]{0:T(1024)}, f32[1024,128]{1,0:T(8,128)}, ...), branch_computations={%region_1.0_spmd, %region_2.7_spmd} | conditional | flops 3640528896 | bytes 23318700 | solution.py:410
  71.6 1.2 %store.1 = (f32[1024,128]{1,0:T(8,128)}, f32[1024,128]{1,0:T(8,128)}, f32[1024,128]{1,0:T(8,128)}) custom-call(f32[1024,128]{1,0:T(8,128)S(1)} %get-tuple-element.18.weights, f32[1024,128]{1,0:T(8,128)S(1)} %get-tuple-element.19.first, f32[1024,128]{1,0:T(8,128)S(1)} %get-tuple-element.20.second), custom_call_target="tpu_custom_call" | custom-call | tf_op jit(solution)/shard_map/cond/branch_0_fun/store/pallas_call | solution.py:397
Async XLA Ops:
  0.6 71.0 %copy-start = (f32[1024,128]{1,0:T(8,128)S(1)}, f32[1024,128]{1,0:T(8,128)}, u32[]{:S(2)}) copy-start(f32[1024,128]{1,0:T(8,128)} %weights_hbm.1) | copy-start | bytes 1572868
  0.6 71.0 %copy-start.1 = (s32[1024,1]{0,1:T(1,128)S(1)}, s32[1024,1]{0,1:T(1,128)}, u32[]{:S(2)}) copy-start(s32[1024,1]{0,1:T(1,128)} %param.9) | copy-start | bytes 12292
